TPU v7x, 32 devices: a whole 2x2x4 slice. The times are simulated.
32 devices in a mesh: beam: 2 (over y), tm: 4 (over z), chan: 2 (over x), pol: 2 (over core).
Axes of the slice: x: 2, y: 2, z: 4, core: 2. Of those that a mesh axis runs over, the one named last changes fastest.
Arguments:
- observed: float32 [2, 2, 64, 4096], P('pol', None, ('beam', 'tm'), 'chan'), parts along dimension 2, may hold values from -18 to 18
- window_taps: float32 [4, 4096], P(None, 'chan'), may hold values from -1.5 to 1.5
Outputs:
- estimate: float32 [2, 2, 64, 4096], P('pol', None, ('beam', 'tm'), 'chan'), parts along dimension 2
- residual: float32 [2, 2, 64, 4096], P('pol', None, ('beam', 'tm'), 'chan'), parts along dimension 2
There are 2 independent parts, one for each index of `beam`. A program takes and returns all parts, laid end to end along the dimension named above; an argument that names none is the same for every part. Nothing has to cross between parts.
All inputs are finite; a program needn't handle non-finite values.
Results may differ from a plain program's by a relative error of at most 0.0003.
Values sent between devices are 32-bit elements; how exact they have to be, the bound alone decides.
A program may use at most 64 MiB of HBM per device.

v0:
```python
import functools
import math

import jax
import jax.numpy as jnp
import ml_dtypes
import numpy as np
from jax import lax
from jax.experimental import pallas as pl
from jax.experimental.pallas import tpu as pltpu
from jax.sharding import PartitionSpec as P

LANES = 128
MESH = pl.DeviceIdType.MESH
F32 = jnp.float32
BF16 = jnp.bfloat16
STATS = 16


def dft_rows(values):
    count = len(values)
    if count == 1:
        return values
    even = dft_rows(values[::2])
    odd = dft_rows(values[1::2])
    low, high = [], []
    for k in range(count // 2):
        er, ei = even[k]
        xr, xi = odd[k]
        if k == 0:
            tr, ti = xr, xi
        elif 4 * k == count:
            tr, ti = -xi, xr
        elif 8 * k == count:
            h = math.sqrt(0.5)
            tr, ti = h * (xr - xi), h * (xr + xi)
        elif 8 * k == 3 * count:
            h = math.sqrt(0.5)
            tr, ti = -h * (xr + xi), h * (xr - xi)
        else:
            cs = math.cos(2 * math.pi * k / count)
            sn = math.sin(2 * math.pi * k / count)
            tr, ti = cs * xr - sn * xi, sn * xr + cs * xi
        low.append((er + tr, ei + ti))
        high.append((er - tr, ei - ti))
    return low + high


def halves(value):
    high = value.astype(BF16)
    return high, (value - high.astype(F32)).astype(BF16)


def dot(left, right):
    return jnp.dot(left, right, preferred_element_type=F32)


def kernel(
    n,
    shards_t,
    obs_ref,
    taps_ref,
    whi_ref,
    wlo_ref,
    tw_ref,
    place_ref,
    perm_ref,
    est_ref,
    res_ref,
    xb,
    hb,
    tb,
    tp,
    zr,
    zi,
    yo,
    yh,
    dd,
    fr,
    es,
    ar,
    sx,
    rx,
    st,
    rt,
    sz,
    rz,
    sa,
    ra,
):
    frames = obs_ref.shape[2]
    taps = taps_ref.shape[0]
    lead = taps - 1
    halo = 2 * lead
    rad = zr.shape[0] // frames
    per = rad // n
    rows = 2 * per
    xs, hs, ts = frames * rows, 2 * halo * rows, taps * per
    c = lax.axis_index("chan")
    t = lax.axis_index("tm")
    has_prev = t > 0
    has_next = t < shards_t - 1

    barrier = pltpu.get_barrier_semaphore()
    for d in range(1, n):
        pl.semaphore_signal(
            barrier, inc=1, device_id={"chan": lax.rem(c + d, n)}, device_id_type=MESH
        )
    for d in range(1, shards_t):
        pl.semaphore_signal(
            barrier, inc=1, device_id={"tm": lax.rem(t + d, shards_t)}, device_id_type=MESH
        )

    for part in range(2):
        for k in range(per):
            xb[pl.ds(c * xs + part * per + k, frames, stride=rows), :] = obs_ref[
                0, part, :, k * LANES : (k + 1) * LANES
            ]
    for k in range(per):
        tb[pl.ds(c * ts + k, taps, stride=per), :] = taps_ref[:, k * LANES : (k + 1) * LANES]

    @pl.when(jnp.logical_not(has_prev))
    def _():
        for j in range(n):
            hb[j * hs : j * hs + halo * rows, :] = jnp.zeros((halo * rows, LANES), F32)

    @pl.when(jnp.logical_not(has_next))
    def _():
        for j in range(n):
            hb[j * hs + halo * rows : (j + 1) * hs, :] = jnp.zeros((halo * rows, LANES), F32)

    pl.semaphore_wait(barrier, n - 1 + shards_t - 1)

    def along_x(d):
        block = xb.at[pl.ds(pl.multiple_of(c * xs, 8), xs), :]
        return pltpu.make_async_remote_copy(
            src_ref=block,
            dst_ref=block,
            send_sem=sx.at[d],
            recv_sem=rx.at[d],
            device_id={"chan": lax.rem(c + d, n)},
            device_id_type=MESH,
        )

    def taps_x(d):
        block = tb.at[pl.ds(pl.multiple_of(c * ts, 8), ts), :]
        return pltpu.make_async_remote_copy(
            src_ref=block,
            dst_ref=block,
            send_sem=st.at[d],
            recv_sem=rt.at[d],
            device_id={"chan": lax.rem(c + d, n)},
            device_id_type=MESH,
        )

    def to_next(d):
        j = lax.rem(c - d + n, n)
        size = halo * rows
        return pltpu.make_async_remote_copy(
            src_ref=xb.at[pl.ds(pl.multiple_of(j * xs + (frames - halo) * rows, 8), size), :],
            dst_ref=hb.at[pl.ds(pl.multiple_of(j * hs, 8), size), :],
            send_sem=sz.at[0, d],
            recv_sem=rz.at[0, d],
            device_id={"tm": lax.rem(t + 1, shards_t)},
            device_id_type=MESH,
        )

    def to_prev(d):
        j = lax.rem(c - d + n, n)
        size = halo * rows
        return pltpu.make_async_remote_copy(
            src_ref=xb.at[pl.ds(pl.multiple_of(j * xs, 8), size), :],
            dst_ref=hb.at[pl.ds(pl.multiple_of(j * hs + size, 8), size), :],
            send_sem=sz.at[1, d],
            recv_sem=rz.at[1, d],
            device_id={"tm": lax.rem(t + shards_t - 1, shards_t)},
            device_id_type=MESH,
        )

    def start_halo(d):
        @pl.when(has_next)
        def _():
            to_next(d).start()

        @pl.when(has_prev)
        def _():
            to_prev(d).start()

    for d in range(1, n):
        along_x(d).start()
    start_halo(0)
    for d in range(1, n):
        taps_x(d).start()
    for d in range(1, n):
        along_x(d).wait_recv()
        start_halo(d)

    def lanes_dft(real, imag):
        hi, lo = halves(jnp.concatenate([real, imag], axis=1))
        whi = whi_ref[...]
        return dot(hi, whi) + dot(lo, whi) + dot(hi, wlo_ref[...])

    def samples(src, stride, first):
        values = []
        for k in range(rad):
            base = (k // per) * stride + first * rows + k % per
            values.append(
                tuple(
                    src[pl.ds(base + part * per, frames, stride=rows), :] for part in range(2)
                )
            )
        for m, (re, im) in enumerate(dft_rows(values)):
            cs, sn = tw_ref[0, m : m + 1, :], tw_ref[1, m : m + 1, :]
            zr[pl.ds(m, frames, stride=rad), :] = re * cs - im * sn
            zi[pl.ds(m, frames, stride=rad), :] = re * sn + im * cs
        return lanes_dft(zr[...], zi[...])

    out = samples(xb, xs, 0)
    yo[0] = out[:, :LANES]
    yo[1] = out[:, LANES:]

    for d in range(1, n):
        taps_x(d).wait_recv()
    turned = tb[...].T
    first = turned.astype(BF16)
    rest = turned - first.astype(F32)
    second = rest.astype(BF16)
    third = (rest - second.astype(F32)).astype(BF16)
    placed = jnp.zeros((rad, taps * LANES), F32)
    for s in range(LANES // rad):
        rng = slice(s * rad, (s + 1) * rad)
        for piece in (third, second, first):
            placed = placed + dot(piece[rng, :], place_ref[s])
    for p in range(taps):
        tp[p * rad : (p + 1) * rad, :] = placed[:, p * LANES : (p + 1) * LANES]

    @pl.when(has_prev)
    def _():
        for d in range(n):
            to_next(d).wait_recv()

    @pl.when(has_next)
    def _():
        for d in range(n):
            to_prev(d).wait_recv()

    shift = 2 * halo - frames

    def halo_step(i, carry):
        begin = i * shift
        out = samples(hb, hs, begin)
        at = pl.ds(pl.multiple_of(begin * rad, 8), frames * rad)
        yh[0, at, :] = out[:, :LANES]
        yh[1, at, :] = out[:, LANES:]
        return carry

    lax.fori_loop(0, 2, halo_step, 0)

    keep_prev = jnp.where(has_prev, 1.0, 0.0).astype(F32)
    keep_next = jnp.where(has_next, 1.0, 0.0).astype(F32)
    chunks = rad // 8

    def window_step(i, carry):
        s0, s1 = carry
        part = i // chunks
        ch = i % chunks

        def at(f):
            return pl.ds(pl.multiple_of(f * rad + ch * 8, 8), 8)

        def signal(f):
            if f < 0:
                return yh[part, at(f + halo), :]
            if f < frames:
                return yo[part, at(f), :]
            return yh[part, at(f - frames + halo), :]

        w = [tp[at(p), :] for p in range(taps)]

        def ahead(x, f):
            return sum(w[p] * x[f + p] for p in range(1, taps)) + w[0] * x[f]

        def behind(x, f):
            return sum(w[p] * x[f - p] for p in range(1, taps)) + w[0] * x[f]

        y = {f: signal(f) for f in range(-halo, frames + halo)}
        g = {f: ahead(y, f) for f in range(-halo, frames + lead)}
        g = {f: (v * keep_prev if f < 0 else v) for f, v in g.items()}
        v = {f: behind(g, f) for f in range(-lead, frames + lead)}
        v = {f: (x * keep_next if f >= frames else x) for f, x in v.items()}
        z = {f: ahead(v, f) for f in range(-lead, frames)}
        z = {f: (x * keep_prev if f < 0 else x) for f, x in z.items()}
        for f in range(frames):
            dd[0, part, at(f), :] = g[f]
            dd[1, part, at(f), :] = z[f]
            dd[2, part, at(f), :] = v[f]
            dd[3, part, at(f), :] = behind(z, f)
            s0 = s0 + g[f] * g[f]
            s1 = s1 + v[f] * v[f]
        return s0, s1

    zero = jnp.zeros((8, LANES), F32)
    s0, s1 = lax.fori_loop(0, 2 * chunks, window_step, (zero, zero))
    s0 = jnp.sum(s0, keepdims=True)
    s1 = jnp.sum(s1, keepdims=True)
    center = jnp.where(s1 > 0, s0 / jnp.where(s1 > 0, s1, 1.0), 0.0)

    def moment_step(i, carry):
        pp, pz, zz, qq, qu, uu = carry
        part = i // chunks
        ch = i % chunks
        for f in range(frames):
            at = pl.ds(pl.multiple_of(f * rad + ch * 8, 8), 8)
            z, u = dd[1, part, at, :], dd[3, part, at, :]
            p = dd[0, part, at, :] - center * z
            q = dd[2, part, at, :] - center * u
            pp, pz, zz = pp + p * p, pz + p * z, zz + z * z
            qq, qu, uu = qq + q * q, qu + q * u, uu + u * u
        return pp, pz, zz, qq, qu, uu

    moments = lax.fori_loop(0, 2 * chunks, moment_step, (zero,) * 6)
    moments = [jnp.sum(x, keepdims=True) for x in moments]
    line = jnp.concatenate(
        [jnp.broadcast_to(x, (1, LANES)) for x in [s0, s1, center] + moments]
        + [jnp.zeros((STATS - 9, LANES), F32)],
        axis=0,
    )
    mine = pl.ds(pl.multiple_of(t * STATS, 8), STATS)
    ar[mine, :] = line

    def sums_to(d):
        return pltpu.make_async_remote_copy(
            src_ref=ar.at[mine, :],
            dst_ref=ar.at[mine, :],
            send_sem=sa.at[d],
            recv_sem=ra.at[d],
            device_id={"tm": lax.rem(t + d, shards_t)},
            device_id_type=MESH,
        )

    for d in range(1, shards_t):
        sums_to(d).start()

    def spectrum_step(a, carry):
        out = lanes_dft(dd[2 + a, 0], -dd[2 + a, 1])
        for f in range(frames):
            at = slice(f * rad, (f + 1) * rad)
            re, im = out[at, :LANES], out[at, LANES:]
            zr[at, :] = re * tw_ref[0] - im * tw_ref[1]
            zi[at, :] = re * tw_ref[1] + im * tw_ref[0]
        values = [
            (zr[pl.ds(m, frames, stride=rad), :], zi[pl.ds(m, frames, stride=rad), :])
            for m in range(rad)
        ]
        for k, (re, im) in enumerate(dft_rows(values)):
            fr[a, 0, k * frames : (k + 1) * frames, :] = re
            fr[a, 1, k * frames : (k + 1) * frames, :] = im
        hi, lo = halves(jnp.concatenate([dd[a, 0], dd[a, 1]], axis=1))
        perm = perm_ref[c]
        moved = dot(hi, perm) + dot(lo, perm)
        quad = LANES // rad
        for h in range(frames // quad):
            flat = moved[h * LANES : (h + 1) * LANES, :].T
            for part in range(2):
                for f in range(quad):
                    joined = jnp.concatenate(
                        [
                            flat[
                                (part * quad + s) * per : (part * quad + s + 1) * per,
                                f * rad : (f + 1) * rad,
                            ]
                            for s in range(quad)
                        ],
                        axis=1,
                    )
                    row = (part * frames + h * quad + f) * per
                    es[a, row : row + per, :] = joined
        return carry

    lax.fori_loop(0, 2, spectrum_step, 0)

    for d in range(1, shards_t):
        sums_to(d).wait_recv()

    def total(i):
        return sum(ar[s * STATS + i : s * STATS + i + 1, :] for s in range(shards_t))

    gamma0 = total(0)
    step0 = gamma0 / total(1)
    gamma1 = jnp.zeros((1, LANES), F32)
    grown = jnp.zeros((1, LANES), F32)
    for s in range(shards_t):
        line = ar[s * STATS : (s + 1) * STATS, :]
        away = step0 - line[2:3]
        gamma1 = gamma1 + (line[3:4] - away * (2.0 * line[4:5] - away * line[5:6]))
        grown = grown + (line[6:7] - away * (2.0 * line[7:8] - away * line[8:9]))
    ratio = gamma1 / gamma0
    step1 = gamma1 / (grown - ratio * gamma1 / step0)
    near = step0 + step1 * (1.0 + ratio)
    far = step0 * step1

    for part in range(2):
        for k in range(per):
            at = pl.ds(pl.multiple_of((c * per + k) * frames, 8), frames)
            change = near * fr[0, part, at, :] - far * fr[1, part, at, :]
            here = obs_ref[0, part, :, k * LANES : (k + 1) * LANES]
            res_ref[0, part, :, k * LANES : (k + 1) * LANES] = (
                here - change if part == 0 else here + change
            )
            at = pl.ds(part * frames * per + k, frames, stride=per)
            est_ref[0, part, :, k * LANES : (k + 1) * LANES] = near * es.at[0][at, :] - far * es.at[
                1
            ][at, :]

    for d in range(1, n):
        along_x(d).wait_send()
        taps_x(d).wait_send()
    for d in range(1, shards_t):
        sums_to(d).wait_send()

    @pl.when(has_next)
    def _():
        for d in range(n):
            to_next(d).wait_send()

    @pl.when(has_prev)
    def _():
        for d in range(n):
            to_prev(d).wait_send()


def tables(n, rad, taps):
    whole = rad * LANES
    index = np.arange(LANES)
    angle = 2.0 * np.pi * (np.outer(index, index) % LANES) / LANES
    cs, sn = np.cos(angle) / math.sqrt(whole), np.sin(angle) / math.sqrt(whole)
    weights = np.block([[cs, sn], [-sn, cs]]).astype(np.float32)
    high = weights.astype(ml_dtypes.bfloat16)
    low = (weights - high.astype(np.float32)).astype(ml_dtypes.bfloat16)
    angle = 2.0 * np.pi * np.outer(np.arange(rad), index) / whole
    twist = np.stack([np.cos(angle), np.sin(angle)]).astype(np.float32)
    per = rad // n
    quad = LANES // rad
    place = np.zeros((quad, taps * rad, taps * LANES), ml_dtypes.bfloat16)
    perm = np.zeros((n, 2 * LANES, 2 * quad * per), ml_dtypes.bfloat16)
    for j in range(n):
        for k in range(per):
            for s in range(quad):
                lane = quad * (j * per + k) + s
                for p in range(taps):
                    place[s, (j * taps + p) * per + k, p * LANES + lane] = 1
                for part in range(2):
                    perm[j, part * LANES + lane, (part * quad + s) * per + k] = 1
    return high, low, twist, place, perm


def shards(n, shards_t, observed, window_taps):
    frames = observed.shape[2]
    taps = window_taps.shape[0]
    rad = observed.shape[3] * n // LANES
    halo = 2 * (taps - 1)
    assert frames == 8 and halo <= frames <= 2 * halo and taps * rad == LANES
    constants = tables(n, rad, taps)
    vmem = pl.BlockSpec(memory_space=pltpu.VMEM)
    dma = pltpu.SemaphoreType.DMA
    return pl.pallas_call(
        functools.partial(kernel, n, shards_t),
        out_shape=(jax.ShapeDtypeStruct(observed.shape, F32),) * 2,
        in_specs=[vmem] * 7,
        out_specs=(vmem, vmem),
        scratch_shapes=[
            pltpu.VMEM((frames * 2 * rad, LANES), F32),
            pltpu.VMEM((2 * halo * 2 * rad, LANES), F32),
            pltpu.VMEM((taps * rad, LANES), F32),
            pltpu.VMEM((taps * rad, LANES), F32),
            pltpu.VMEM((frames * rad, LANES), F32),
            pltpu.VMEM((frames * rad, LANES), F32),
            pltpu.VMEM((2, frames * rad, LANES), F32),
            pltpu.VMEM((2, 2 * halo * rad, LANES), F32),
            pltpu.VMEM((4, 2, frames * rad, LANES), F32),
            pltpu.VMEM((2, 2, frames * rad, LANES), F32),
            pltpu.VMEM((2, 2 * frames * rad // n, LANES), F32),
            pltpu.VMEM((shards_t * STATS, LANES), F32),
            dma((n,)),
            dma((n,)),
            dma((n,)),
            dma((n,)),
            dma((2, n)),
            dma((2, n)),
            dma((shards_t,)),
            dma((shards_t,)),
        ],
        compiler_params=pltpu.CompilerParams(
            collective_id=0, has_side_effects=True, vmem_limit_bytes=32 * 1024 * 1024
        ),
        cost_estimate=pl.CostEstimate(flops=10**9, bytes_accessed=10**6, transcendentals=0),
    )(observed, window_taps, *(jnp.asarray(x) for x in constants))


def solution(mesh):
    n, shards_t = mesh.shape["chan"], mesh.shape["tm"]
    block = P("pol", None, ("beam", "tm"), "chan")
    return jax.shard_map(
        functools.partial(shards, n, shards_t),
        mesh=mesh,
        in_specs=(block, P(None, "chan")),
        out_specs=(block, block),
        check_vma=False,
    )
```

profile of v0, /device:TPU:0, one launch (start us, length us, event | category | flops | bytes accessed | tf_op | source)
XLA Modules:
  0.0 27.2 jit_solution(2996365958705374216)
XLA Ops:
  0.6 0.0 copy-start
  0.6 0.9 %copy-done = f32[1,2,8,2048]{3,2,1,0:T(8,128)S(1)} copy-done((f32[1,2,8,2048]{3,2,1,0:T(8,128)S(1)}, f32[1,2,8,2048]{3,2,1,0:T(8,128)}, u32[]{:S(2)}) %copy-start) | copy-done | bytes 131096
  1.5 0.0 copy-start.1
  1.5 0.8 %copy-done.1 = f32[4,2048]{1,0:T(4,128)S(1)} copy-done((f32[4,2048]{1,0:T(4,128)S(1)}, f32[4,2048]{1,0:T(4,128)}, u32[]{:S(2)}) %copy-start.1) | copy-done | bytes 32792
  2.3 0.0 copy-start.2
  2.3 1.0 %copy-done.2 = bf16[4,128,512]{2,1,0:T(8,128)(2,1)S(1)} copy-done((bf16[4,128,512]{2,1,0:T(8,128)(2,1)S(1)}, bf16[4,128,512]{2,1,0:T(8,128)(2,1)}, u32[]{:S(2)}) %copy-start.2) | copy-done | bytes 524312
  3.3 0.0 copy-start.3
  3.3 0.9 %copy-done.3 = bf16[2,256,128]{2,1,0:T(8,128)(2,1)S(1)} copy-done((bf16[2,256,128]{2,1,0:T(8,128)(2,1)S(1)}, bf16[2,256,128]{2,1,0:T(8,128)(2,1)}, u32[]{:S(2)}) %copy-start.3) | copy-done | bytes 131096
  4.2 0.0 copy-start.4
  4.2 0.9 %copy-done.4 = bf16[256,256]{1,0:T(8,128)(2,1)S(1)} copy-done((bf16[256,256]{1,0:T(8,128)(2,1)S(1)}, bf16[256,256]{1,0:T(8,128)(2,1)}, u32[]{:S(2)}) %copy-start.4) | copy-done | bytes 131096
  5.1 0.0 copy-start.5
  5.1 0.9 %copy-done.5 = bf16[256,256]{1,0:T(8,128)(2,1)S(1)} copy-done((bf16[256,256]{1,0:T(8,128)(2,1)S(1)}, bf16[256,256]{1,0:T(8,128)(2,1)}, u32[]{:S(2)}) %copy-start.5) | copy-done | bytes 131096
  6.0 0.0 copy-start.6
  6.1 0.8 %copy-done.6 = f32[2,32,128]{2,1,0:T(8,128)S(1)} copy-done((f32[2,32,128]{2,1,0:T(8,128)S(1)}, f32[2,32,128]{2,1,0:T(8,128)}, u32[]{:S(2)}) %copy-start.6) | copy-done | bytes 32792
  6.8 19.1 %shard_map.86 = (f32[1,2,8,2048]{3,2,1,0:T(8,128)S(1)}, f32[1,2,8,2048]{3,2,1,0:T(8,128)S(1)}) custom-call(f32[1,2,8,2048]{3,2,1,0:T(8,128)S(1)} %copy-done, f32[4,2048]{1,0:T(4,128)S(1)} %copy-done.1, bf16[256,256]{1,0:T(8,128)(2,1)S(1)} %copy-done.5, bf16[256,256]{1,0:T(8,128)(2,1)S(1)} %copy-done.4, f32[2,32,128]{2,1,0:T(8,128)S(1)} %copy-done.6, ...), custom_call_target="tpu_custom_call" | custom-call | flops 1000000000 | bytes 1000000 | tf_op jit(solution)/shard_map/pallas_call | solution.py:466
  25.9 0.7 %copy.11 = f32[1,2,8,2048]{3,2,1,0:T(8,128)} copy(f32[1,2,8,2048]{3,2,1,0:T(8,128)S(1)} %get-tuple-element.4) | data formatting | bytes 262144
  26.6 0.7 %copy.12 = f32[1,2,8,2048]{3,2,1,0:T(8,128)} copy(f32[1,2,8,2048]{3,2,1,0:T(8,128)S(1)} %get-tuple-element.5) | data formatting | bytes 262144
Async XLA Ops:
  0.6 0.9 %copy-start = (f32[1,2,8,2048]{3,2,1,0:T(8,128)S(1)}, f32[1,2,8,2048]{3,2,1,0:T(8,128)}, u32[]{:S(2)}) copy-start(f32[1,2,8,2048]{3,2,1,0:T(8,128)} %obs_ref.1) | copy-start | bytes 393220
  1.5 0.8 %copy-start.1 = (f32[4,2048]{1,0:T(4,128)S(1)}, f32[4,2048]{1,0:T(4,128)}, u32[]{:S(2)}) copy-start(f32[4,2048]{1,0:T(4,128)} %taps_ref.1) | copy-start | bytes 98308
  2.3 1.0 %copy-start.2 = (bf16[4,128,512]{2,1,0:T(8,128)(2,1)S(1)}, bf16[4,128,512]{2,1,0:T(8,128)(2,1)}, u32[]{:S(2)}) copy-start(bf16[4,128,512]{2,1,0:T(8,128)(2,1)} %constant.13.clone.place_ref) | copy-start | bytes 1572868
  3.3 0.9 %copy-start.3 = (bf16[2,256,128]{2,1,0:T(8,128)(2,1)S(1)}, bf16[2,256,128]{2,1,0:T(8,128)(2,1)}, u32[]{:S(2)}) copy-start(bf16[2,256,128]{2,1,0:T(8,128)(2,1)} %constant.14.clone.perm_ref) | copy-start | bytes 393220
  4.2 0.9 %copy-start.4 = (bf16[256,256]{1,0:T(8,128)(2,1)S(1)}, bf16[256,256]{1,0:T(8,128)(2,1)}, u32[]{:S(2)}) copy-start(bf16[256,256]{1,0:T(8,128)(2,1)} %constant.11.clone.wlo_ref) | copy-start | bytes 393220
  5.1 0.9 %copy-start.5 = (bf16[256,256]{1,0:T(8,128)(2,1)S(1)}, bf16[256,256]{1,0:T(8,128)(2,1)}, u32[]{:S(2)}) copy-start(bf16[256,256]{1,0:T(8,128)(2,1)} %constant.10.clone.whi_ref) | copy-start | bytes 393220
  6.0 0.8 %copy-start.6 = (f32[2,32,128]{2,1,0:T(8,128)S(1)}, f32[2,32,128]{2,1,0:T(8,128)}, u32[]{:S(2)}) copy-start(f32[2,32,128]{2,1,0:T(8,128)} %constant.12.clone.tw_ref) | copy-start | bytes 98308
where the time goes:
time: 27.6 us; the launch traced here: 27.2 us
  Pallas kernels  19.1 us (69%)
  local copies, waits for them, and re-layouts  7.48 us (27%)
  between operations  0.65 us (2%)
    pallas_call x1, Pallas kernels, shards(): pl.pallas_call(functools.partial(kernel, n, shards_t), out_shape=(jax.Sha...  19.1 us
    unnamed x16, local copies, waits for them, and re-layouts  7.48 us

commit v1 on v0

--- a/solution.py
+++ b/solution.py
@@ -58,6 +58,15 @@
 def kernel(
     n,
     shards_t,
+    obs_hbm,
+    taps_hbm,
+    whi_hbm,
+    wlo_hbm,
+    tw_hbm,
+    place_hbm,
+    perm_hbm,
+    est_ref,
+    res_ref,
     obs_ref,
     taps_ref,
     whi_ref,
@@ -65,8 +74,7 @@
     tw_ref,
     place_ref,
     perm_ref,
-    est_ref,
-    res_ref,
+    lo,
     xb,
     hb,
     tb,
@@ -88,6 +96,22 @@
     sa,
     ra,
 ):
+    loads = [
+        pltpu.make_async_copy(src, dst, lo.at[i])
+        for i, (src, dst) in enumerate(
+            [
+                (obs_hbm, obs_ref),
+                (taps_hbm, taps_ref),
+                (tw_hbm, tw_ref),
+                (whi_hbm, whi_ref),
+                (wlo_hbm, wlo_ref),
+                (place_hbm, place_ref),
+                (perm_hbm, perm_ref),
+            ]
+        )
+    ]
+    for load in loads:
+        load.start()
     frames = obs_ref.shape[2]
     taps = taps_ref.shape[0]
     lead = taps - 1
@@ -95,6 +119,8 @@
     rad = zr.shape[0] // frames
     per = rad // n
     rows = 2 * per
+    step = frames - halo
+    pieces = [*range(step, frames - step, step), 0, frames - step]
     xs, hs, ts = frames * rows, 2 * halo * rows, taps * per
     c = lax.axis_index("chan")
     t = lax.axis_index("tm")
@@ -111,11 +137,13 @@
             barrier, inc=1, device_id={"tm": lax.rem(t + d, shards_t)}, device_id_type=MESH
         )
 
+    loads[0].wait()
     for part in range(2):
         for k in range(per):
             xb[pl.ds(c * xs + part * per + k, frames, stride=rows), :] = obs_ref[
                 0, part, :, k * LANES : (k + 1) * LANES
             ]
+    loads[1].wait()
     for k in range(per):
         tb[pl.ds(c * ts + k, taps, stride=per), :] = taps_ref[:, k * LANES : (k + 1) * LANES]
 
@@ -131,13 +159,13 @@
 
     pl.semaphore_wait(barrier, n - 1 + shards_t - 1)
 
-    def along_x(d):
-        block = xb.at[pl.ds(pl.multiple_of(c * xs, 8), xs), :]
+    def along_x(d, q):
+        block = xb.at[pl.ds(pl.multiple_of(c * xs + pieces[q] * rows, 8), step * rows), :]
         return pltpu.make_async_remote_copy(
             src_ref=block,
             dst_ref=block,
-            send_sem=sx.at[d],
-            recv_sem=rx.at[d],
+            send_sem=sx.at[d, q],
+            recv_sem=rx.at[d, q],
             device_id={"chan": lax.rem(c + d, n)},
             device_id_type=MESH,
         )
@@ -153,47 +181,51 @@
             device_id_type=MESH,
         )
 
-    def to_next(d):
+    def along_z(way, d, q, first, last):
         j = lax.rem(c - d + n, n)
-        size = halo * rows
+        slot = first - (frames - halo) if way == 0 else halo + first
+        size = (last - first) * rows
         return pltpu.make_async_remote_copy(
-            src_ref=xb.at[pl.ds(pl.multiple_of(j * xs + (frames - halo) * rows, 8), size), :],
-            dst_ref=hb.at[pl.ds(pl.multiple_of(j * hs, 8), size), :],
-            send_sem=sz.at[0, d],
-            recv_sem=rz.at[0, d],
-            device_id={"tm": lax.rem(t + 1, shards_t)},
+            src_ref=xb.at[pl.ds(pl.multiple_of(j * xs + first * rows, 8), size), :],
+            dst_ref=hb.at[pl.ds(pl.multiple_of(j * hs + slot * rows, 8), size), :],
+            send_sem=sz.at[way, d, q],
+            recv_sem=rz.at[way, d, q],
+            device_id={"tm": lax.rem(t + (1 if way == 0 else shards_t - 1), shards_t)},
             device_id_type=MESH,
         )
 
-    def to_prev(d):
-        j = lax.rem(c - d + n, n)
-        size = halo * rows
-        return pltpu.make_async_remote_copy(
-            src_ref=xb.at[pl.ds(pl.multiple_of(j * xs, 8), size), :],
-            dst_ref=hb.at[pl.ds(pl.multiple_of(j * hs + size, 8), size), :],
-            send_sem=sz.at[1, d],
-            recv_sem=rz.at[1, d],
-            device_id={"tm": lax.rem(t + shards_t - 1, shards_t)},
-            device_id_type=MESH,
-        )
-
-    def start_halo(d):
-        @pl.when(has_next)
-        def _():
-            to_next(d).start()
-
-        @pl.when(has_prev)
-        def _():
-            to_prev(d).start()
-
-    for d in range(1, n):
-        along_x(d).start()
-    start_halo(0)
+    spans = ((frames - halo, frames), (0, halo))
+    forward = [[], []]
+    for way in range(2):
+        forward[way].append((0, 0) + spans[way])
+        for d in range(1, n):
+            for q, f in enumerate(pieces):
+                if spans[way][0] <= f < spans[way][1]:
+                    forward[way].append((d, q, f, f + step))
+    sends_to = (has_next, has_prev)
+    gets_from = (has_prev, has_next)
+
+    def start_halo(d, q):
+        for way in range(2):
+            for move in forward[way]:
+                if move[:2] == (d, q):
+
+                    @pl.when(sends_to[way])
+                    def _(way=way, move=move):
+                        along_z(way, *move).start()
+
+    for q in range(len(pieces)):
+        for d in range(1, n):
+            along_x(d, q).start()
+    start_halo(0, 0)
+    for load in loads[2:]:
+        load.wait()
+    for q in range(len(pieces)):
+        for d in range(1, n):
+            along_x(d, q).wait_recv()
+            start_halo(d, q)
     for d in range(1, n):
         taps_x(d).start()
-    for d in range(1, n):
-        along_x(d).wait_recv()
-        start_halo(d)
 
     def lanes_dft(real, imag):
         hi, lo = halves(jnp.concatenate([real, imag], axis=1))
@@ -234,15 +266,12 @@
     for p in range(taps):
         tp[p * rad : (p + 1) * rad, :] = placed[:, p * LANES : (p + 1) * LANES]
 
-    @pl.when(has_prev)
-    def _():
-        for d in range(n):
-            to_next(d).wait_recv()
-
-    @pl.when(has_next)
-    def _():
-        for d in range(n):
-            to_prev(d).wait_recv()
+    for way in range(2):
+
+        @pl.when(gets_from[way])
+        def _(way=way):
+            for move in forward[way]:
+                along_z(way, *move).wait_recv()
 
     shift = 2 * halo - frames
 
@@ -413,20 +442,37 @@
             ][at, :]
 
     for d in range(1, n):
-        along_x(d).wait_send()
+        for q in range(len(pieces)):
+            along_x(d, q).wait_send()
         taps_x(d).wait_send()
     for d in range(1, shards_t):
         sums_to(d).wait_send()
-
-    @pl.when(has_next)
-    def _():
-        for d in range(n):
-            to_next(d).wait_send()
-
-    @pl.when(has_prev)
-    def _():
-        for d in range(n):
-            to_prev(d).wait_send()
+    for way in range(2):
+
+        @pl.when(sends_to[way])
+        def _(way=way):
+            for move in forward[way]:
+                along_z(way, *move).wait_send()
+
+
+def place_results(est_in, res_in, est_out, res_out, est_buf, res_buf, sems):
+    moves = []
+    for src, buf, dst in ((est_in, est_buf, est_out), (res_in, res_buf, res_out)):
+        for part in range(2):
+            i = len(moves)
+            moves.append(
+                (
+                    pltpu.make_async_copy(src.at[0, part], buf.at[part], sems.at[0, i]),
+                    pltpu.make_async_copy(buf.at[part], dst.at[0, part], sems.at[1, i]),
+                )
+            )
+    for load, _ in moves:
+        load.start()
+    for load, store in moves:
+        load.wait()
+        store.start()
+    for _, store in moves:
+        store.wait()
 
 
 def tables(n, rad, taps):
@@ -461,14 +507,19 @@
     halo = 2 * (taps - 1)
     assert frames == 8 and halo <= frames <= 2 * halo and taps * rad == LANES
     constants = tables(n, rad, taps)
+    hbm = pl.BlockSpec(memory_space=pltpu.HBM)
     vmem = pl.BlockSpec(memory_space=pltpu.VMEM)
     dma = pltpu.SemaphoreType.DMA
-    return pl.pallas_call(
+    results = pl.pallas_call(
         functools.partial(kernel, n, shards_t),
         out_shape=(jax.ShapeDtypeStruct(observed.shape, F32),) * 2,
-        in_specs=[vmem] * 7,
+        in_specs=[hbm] * 7,
         out_specs=(vmem, vmem),
         scratch_shapes=[
+            pltpu.VMEM(observed.shape, F32),
+            pltpu.VMEM(window_taps.shape, F32),
+            *(pltpu.VMEM(constants[i].shape, constants[i].dtype) for i in (0, 1, 2, 3, 4)),
+            dma((7,)),
             pltpu.VMEM((frames * 2 * rad, LANES), F32),
             pltpu.VMEM((2 * halo * 2 * rad, LANES), F32),
             pltpu.VMEM((taps * rad, LANES), F32),
@@ -481,20 +532,32 @@
             pltpu.VMEM((2, 2, frames * rad, LANES), F32),
             pltpu.VMEM((2, 2 * frames * rad // n, LANES), F32),
             pltpu.VMEM((shards_t * STATS, LANES), F32),
+            dma((n, frames // 2)),
+            dma((n, frames // 2)),
             dma((n,)),
             dma((n,)),
-            dma((n,)),
-            dma((n,)),
-            dma((2, n)),
-            dma((2, n)),
+            dma((2, n, frames // 2)),
+            dma((2, n, frames // 2)),
             dma((shards_t,)),
             dma((shards_t,)),
         ],
         compiler_params=pltpu.CompilerParams(
-            collective_id=0, has_side_effects=True, vmem_limit_bytes=32 * 1024 * 1024
+            collective_id=0, has_side_effects=True, vmem_limit_bytes=56 * 1024 * 1024
         ),
         cost_estimate=pl.CostEstimate(flops=10**9, bytes_accessed=10**6, transcendentals=0),
     )(observed, window_taps, *(jnp.asarray(x) for x in constants))
+    return pl.pallas_call(
+        place_results,
+        out_shape=(jax.ShapeDtypeStruct(observed.shape, F32),) * 2,
+        in_specs=[hbm] * 2,
+        out_specs=(hbm, hbm),
+        scratch_shapes=[
+            pltpu.VMEM(observed.shape[1:], F32),
+            pltpu.VMEM(observed.shape[1:], F32),
+            dma((2, 4)),
+        ],
+        compiler_params=pltpu.CompilerParams(vmem_limit_bytes=56 * 1024 * 1024),
+    )(*results)
 
 
 def solution(mesh):

time: 27.6 us -> 22 us (0.80)
  local copies, waits for them, and re-layouts: 7.48 us -> 0 us
  Pallas kernels: 19.1 us -> 21.1 us
    unnamed x16 -> x0, local copies, waits for them, and re-layouts: 7.48 us -> none
    pallas_call x0 -> x1, Pallas kernels: none -> 1.63 us  [shards(): pl.pallas_call(place_results, out_shape=(jax.ShapeDtypeStruct(observed.sh...]
    pallas_call x1, Pallas kernels: 19.1 us -> 19.5 us  [shards(): pl.pallas_call(functools.partial(kernel, n, shards_t), out_shape=(jax.Sha...]
where the time goes in v1:
time: 22 us; the launch traced here: 21.8 us
  Pallas kernels  21.1 us (96%)
  between operations  0.64 us (3%)
    pallas_call x1, Pallas kernels, shards(): pl.pallas_call(functools.partial(kernel, n, shards_t), out_shape=(jax.Sha...  19.5 us
    pallas_call x1, Pallas kernels, shards(): pl.pallas_call(place_results, out_shape=(jax.ShapeDtypeStruct(observed.sh...  1.63 us

profile of v1, /device:TPU:0, one launch (start us, length us, event | category | flops | bytes accessed | tf_op | source)
XLA Modules:
  0.0 21.8 jit_solution(13384923905462011576)
XLA Ops:
  0.6 19.5 %shard_map.86 = (f32[1,2,8,2048]{3,2,1,0:T(8,128)}, f32[1,2,8,2048]{3,2,1,0:T(8,128)}) custom-call(f32[1,2,8,2048]{3,2,1,0:T(8,128)} %obs_hbm.1, f32[4,2048]{1,0:T(4,128)} %taps_hbm.1, bf16[256,256]{1,0:T(8,128)(2,1)} %constant.10.clone.whi_hbm, bf16[256,256]{1,0:T(8,128)(2,1)} %constant.11.clone.wlo_hbm, f32[2,32,128]{2,1,0:T(8,128)} %constant.12.clone.tw_hbm, ...), custom_call_target="tpu_custom_call" | custom-call | flops 1000000000 | bytes 1000000 | tf_op jit(solution)/shard_map/pallas_call | solution.py:513
  20.1 1.6 %shard_map.87 = (f32[1,2,8,2048]{3,2,1,0:T(8,128)}, f32[1,2,8,2048]{3,2,1,0:T(8,128)}) custom-call(f32[1,2,8,2048]{3,2,1,0:T(8,128)} %get-tuple-element.4.est_in, f32[1,2,8,2048]{3,2,1,0:T(8,128)} %get-tuple-element.5.res_in), custom_call_target="tpu_custom_call" | custom-call | tf_op jit(solution)/shard_map/pallas_call | solution.py:549

commit v2 on v1

--- a/solution.py
+++ b/solution.py
@@ -102,7 +102,7 @@
             [
                 (obs_hbm, obs_ref),
                 (taps_hbm, taps_ref),
-                (tw_hbm, tw_ref),
+                (tw_hbm.at[:, : tw_ref.shape[1]], tw_ref),
                 (whi_hbm, whi_ref),
                 (wlo_hbm, wlo_ref),
                 (place_hbm, place_ref),
@@ -218,15 +218,14 @@
         for d in range(1, n):
             along_x(d, q).start()
     start_halo(0, 0)
+    for d in range(1, n):
+        taps_x(d).start()
     for load in loads[2:]:
         load.wait()
     for q in range(len(pieces)):
         for d in range(1, n):
             along_x(d, q).wait_recv()
             start_halo(d, q)
-    for d in range(1, n):
-        taps_x(d).start()
-
     def lanes_dft(real, imag):
         hi, lo = halves(jnp.concatenate([real, imag], axis=1))
         whi = whi_ref[...]
@@ -455,24 +454,16 @@
                 along_z(way, *move).wait_send()
 
 
-def place_results(est_in, res_in, est_out, res_out, est_buf, res_buf, sems):
-    moves = []
-    for src, buf, dst in ((est_in, est_buf, est_out), (res_in, res_buf, res_out)):
-        for part in range(2):
-            i = len(moves)
-            moves.append(
-                (
-                    pltpu.make_async_copy(src.at[0, part], buf.at[part], sems.at[0, i]),
-                    pltpu.make_async_copy(buf.at[part], dst.at[0, part], sems.at[1, i]),
-                )
-            )
-    for load, _ in moves:
-        load.start()
-    for load, store in moves:
-        load.wait()
-        store.start()
-    for _, store in moves:
-        store.wait()
+def place_results(est_in, res_in, est_out, res_out, sems):
+    moves = [
+        pltpu.make_async_copy(src.at[:, part], dst.at[:, part], sems.at[2 * i + part])
+        for i, (src, dst) in enumerate([(est_in, est_out), (res_in, res_out)])
+        for part in range(2)
+    ]
+    for move in moves:
+        move.start()
+    for move in moves:
+        move.wait()
 
 
 def tables(n, rad, taps):
@@ -507,6 +498,9 @@
     halo = 2 * (taps - 1)
     assert frames == 8 and halo <= frames <= 2 * halo and taps * rad == LANES
     constants = tables(n, rad, taps)
+    shapes = [x.shape for x in constants]
+    constants = list(constants)
+    constants[2] = np.pad(constants[2], ((0, 0), (0, 1024), (0, 0)))
     hbm = pl.BlockSpec(memory_space=pltpu.HBM)
     vmem = pl.BlockSpec(memory_space=pltpu.VMEM)
     dma = pltpu.SemaphoreType.DMA
@@ -518,7 +512,7 @@
         scratch_shapes=[
             pltpu.VMEM(observed.shape, F32),
             pltpu.VMEM(window_taps.shape, F32),
-            *(pltpu.VMEM(constants[i].shape, constants[i].dtype) for i in (0, 1, 2, 3, 4)),
+            *(pltpu.VMEM(shapes[i], constants[i].dtype) for i in (0, 1, 2, 3, 4)),
             dma((7,)),
             pltpu.VMEM((frames * 2 * rad, LANES), F32),
             pltpu.VMEM((2 * halo * 2 * rad, LANES), F32),
@@ -542,21 +536,19 @@
             dma((shards_t,)),
         ],
         compiler_params=pltpu.CompilerParams(
-            collective_id=0, has_side_effects=True, vmem_limit_bytes=56 * 1024 * 1024
+            collective_id=0, has_side_effects=True, vmem_limit_bytes=56229888
         ),
         cost_estimate=pl.CostEstimate(flops=10**9, bytes_accessed=10**6, transcendentals=0),
     )(observed, window_taps, *(jnp.asarray(x) for x in constants))
     return pl.pallas_call(
         place_results,
         out_shape=(jax.ShapeDtypeStruct(observed.shape, F32),) * 2,
-        in_specs=[hbm] * 2,
+        in_specs=[vmem] * 2,
         out_specs=(hbm, hbm),
         scratch_shapes=[
-            pltpu.VMEM(observed.shape[1:], F32),
-            pltpu.VMEM(observed.shape[1:], F32),
-            dma((2, 4)),
+            dma((4,)),
         ],
-        compiler_params=pltpu.CompilerParams(vmem_limit_bytes=56 * 1024 * 1024),
+        compiler_params=pltpu.CompilerParams(vmem_limit_bytes=4 * 1024 * 1024),
     )(*results)
 
 

time: 22 us -> 21.2 us (0.964)
  Pallas kernels: 21.1 us -> 19.6 us
  local copies, waits for them, and re-layouts: 0 us -> 0.75 us
    pallas_call x1, Pallas kernels: 1.63 us -> 0.73 us  [shards(): pl.pallas_call(place_results, out_shape=(jax.ShapeDtypeStruct(observed.sh...]
    unnamed x0 -> x2, local copies, waits for them, and re-layouts: none -> 0.75 us
    pallas_call x1, Pallas kernels: 19.5 us -> 18.9 us  [shards(): pl.pallas_call(functools.partial(kernel, n, shards_t), out_shape=(jax.Sha...]
where the time goes in v2:
time: 21.2 us; the launch traced here: 21 us
  Pallas kernels  19.6 us (92%)
  local copies, waits for them, and re-layouts  0.75 us (4%)
  between operations  0.65 us (3%)
    pallas_call x1, Pallas kernels, shards(): pl.pallas_call(functools.partial(kernel, n, shards_t), out_shape=(jax.Sha...  18.9 us
    unnamed x2, local copies, waits for them, and re-layouts  0.75 us
    pallas_call x1, Pallas kernels, shards(): pl.pallas_call(place_results, out_shape=(jax.ShapeDtypeStruct(observed.sh...  0.73 us

profile of v2, /device:TPU:0, one launch (start us, length us, event | category | flops | bytes accessed | tf_op | source)
XLA Modules:
  0.0 21.0 jit_solution(13922726654941117365)
XLA Ops:
  0.6 0.0 copy-start
  0.6 0.7 %copy-done = f32[4,2048]{1,0:T(4,128)S(1)} copy-done((f32[4,2048]{1,0:T(4,128)S(1)}, f32[4,2048]{1,0:T(4,128)}, u32[]{:S(2)}) %copy-start) | copy-done | bytes 32792
  1.4 18.9 %shard_map.86 = (f32[1,2,8,2048]{3,2,1,0:T(8,128)S(1)}, f32[1,2,8,2048]{3,2,1,0:T(8,128)S(1)}) custom-call(f32[1,2,8,2048]{3,2,1,0:T(8,128)} %obs_hbm.1, f32[4,2048]{1,0:T(4,128)S(1)} %copy-done, bf16[256,256]{1,0:T(8,128)(2,1)} %constant.10.clone.whi_hbm, bf16[256,256]{1,0:T(8,128)(2,1)} %constant.11.clone.wlo_hbm, f32[2,1056,128]{2,1,0:T(8,128)} %constant.12.clone.tw_hbm, ...), custom_call_target="tpu_custom_call" | custom-call | flops 1000000000 | bytes 1000000 | tf_op jit(solution)/shard_map/pallas_call | solution.py:507
  20.3 0.7 %shard_map.87 = (f32[1,2,8,2048]{3,2,1,0:T(8,128)}, f32[1,2,8,2048]{3,2,1,0:T(8,128)}) custom-call(f32[1,2,8,2048]{3,2,1,0:T(8,128)S(1)} %get-tuple-element.4.est_in, f32[1,2,8,2048]{3,2,1,0:T(8,128)S(1)} %get-tuple-element.5.res_in), custom_call_target="tpu_custom_call" | custom-call | tf_op jit(solution)/shard_map/pallas_call | solution.py:543
Async XLA Ops:
  0.6 0.8 %copy-start = (f32[4,2048]{1,0:T(4,128)S(1)}, f32[4,2048]{1,0:T(4,128)}, u32[]{:S(2)}) copy-start(f32[4,2048]{1,0:T(4,128)} %taps_hbm.1) | copy-start | bytes 98308

commit v3 on v2

--- a/solution.py
+++ b/solution.py
@@ -536,7 +536,7 @@
             dma((shards_t,)),
         ],
         compiler_params=pltpu.CompilerParams(
-            collective_id=0, has_side_effects=True, vmem_limit_bytes=56229888
+            collective_id=0, has_side_effects=True, vmem_limit_bytes=56262656
         ),
         cost_estimate=pl.CostEstimate(flops=10**9, bytes_accessed=10**6, transcendentals=0),
     )(observed, window_taps, *(jnp.asarray(x) for x in constants))

time: 21.2 us -> 21.2 us (level)
  no operation moved by 1% of the time
where the time goes in v3:
time: 21.2 us; the launch traced here: 21 us
  Pallas kernels  19.6 us (92%)
  local copies, waits for them, and re-layouts  0.75 us (4%)
  between operations  0.65 us (3%)
    pallas_call x1, Pallas kernels, shards(): pl.pallas_call(functools.partial(kernel, n, shards_t), out_shape=(jax.Sha...  18.9 us
    unnamed x2, local copies, waits for them, and re-layouts  0.75 us
    pallas_call x1, Pallas kernels, shards(): pl.pallas_call(place_results, out_shape=(jax.ShapeDtypeStruct(observed.sh...  0.73 us

profile of v3, /device:TPU:0, one launch (start us, length us, event | category | flops | bytes accessed | tf_op | source)
XLA Modules:
  0.0 21.0 jit_solution(9494373863510542490)
XLA Ops:
  0.6 0.0 copy-start
  0.6 0.7 %copy-done = f32[4,2048]{1,0:T(4,128)S(1)} copy-done((f32[4,2048]{1,0:T(4,128)S(1)}, f32[4,2048]{1,0:T(4,128)}, u32[]{:S(2)}) %copy-start) | copy-done | bytes 32792
  1.4 18.9 %shard_map.86 = (f32[1,2,8,2048]{3,2,1,0:T(8,128)S(1)}, f32[1,2,8,2048]{3,2,1,0:T(8,128)S(1)}) custom-call(f32[1,2,8,2048]{3,2,1,0:T(8,128)} %obs_hbm.1, f32[4,2048]{1,0:T(4,128)S(1)} %copy-done, bf16[256,256]{1,0:T(8,128)(2,1)} %constant.10.clone.whi_hbm, bf16[256,256]{1,0:T(8,128)(2,1)} %constant.11.clone.wlo_hbm, f32[2,1056,128]{2,1,0:T(8,128)} %constant.12.clone.tw_hbm, ...), custom_call_target="tpu_custom_call" | custom-call | flops 1000000000 | bytes 1000000 | tf_op jit(solution)/shard_map/pallas_call | solution.py:507
  20.3 0.7 %shard_map.87 = (f32[1,2,8,2048]{3,2,1,0:T(8,128)}, f32[1,2,8,2048]{3,2,1,0:T(8,128)}) custom-call(f32[1,2,8,2048]{3,2,1,0:T(8,128)S(1)} %get-tuple-element.4.est_in, f32[1,2,8,2048]{3,2,1,0:T(8,128)S(1)} %get-tuple-element.5.res_in), custom_call_target="tpu_custom_call" | custom-call | tf_op jit(solution)/shard_map/pallas_call | solution.py:543
Async XLA Ops:
  0.6 0.8 %copy-start = (f32[4,2048]{1,0:T(4,128)S(1)}, f32[4,2048]{1,0:T(4,128)}, u32[]{:S(2)}) copy-start(f32[4,2048]{1,0:T(4,128)} %taps_hbm.1) | copy-start | bytes 98308
